TPU v7x, 256 devices: a whole 4x4x8 slice. The times are simulated.
256 devices in a mesh: dp: 4 (over x), fsdp: 4 (over z_hi), row: 16 (over y, z_lo, core).
Axes of the slice: x: 4, y: 4, z: 8 (z_hi: 4, z_lo: 2; z = z_hi * 2 + z_lo), core: 2. Of those that a mesh axis runs over, the one named last changes fastest.
Arguments:
- patches: bfloat16 [16, 32, 128, 2048], P(('dp', 'fsdp'), 'row'), may hold values from -6 to 6
- q_rows: bfloat16 [16, 32, 128, 1024], P(('dp', 'fsdp'), 'row'), may hold values from -4.5 to 4.5
- k_rows: bfloat16 [16, 32, 128, 1024], P(('dp', 'fsdp'), 'row'), may hold values from -4.5 to 4.5
- v_rows: bfloat16 [16, 32, 128, 1024], P(('dp', 'fsdp'), 'row'), may hold values from -6 to 6
- w_out: bfloat16 [1024, 2048], P(('fsdp', 'row')), may hold values from -0.1875 to 0.1875
- gain: bfloat16 [2048], replicated, may hold values from 0.099609375 to 1.8984375
- w_val: bfloat16 [2048, 1024], P(('fsdp', 'row')), may hold values from -0.125 to 0.125
- q_cols: bfloat16 [16, 32, 128, 1024], P(('dp', 'fsdp'), None, 'row'), may hold values from -4.5 to 4.5
- k_cols: bfloat16 [16, 32, 128, 1024], P(('dp', 'fsdp'), None, 'row'), may hold values from -4.5 to 4.5
- cotangent: bfloat16 [16, 32, 128, 1024], P(('dp', 'fsdp'), None, 'row'), may hold values from -6 to 6
Outputs:
- grad_patches: bfloat16 [16, 32, 128, 2048], P(('dp', 'fsdp'), 'row')
- grad_q_rows: bfloat16 [16, 32, 128, 1024], P(('dp', 'fsdp'), 'row')
- grad_k_rows: bfloat16 [16, 32, 128, 1024], P(('dp', 'fsdp'), 'row')
- grad_v_rows: bfloat16 [16, 32, 128, 1024], P(('dp', 'fsdp'), 'row')
- grad_q_cols: bfloat16 [16, 32, 128, 1024], P(('dp', 'fsdp'), None, 'row')
- grad_k_cols: bfloat16 [16, 32, 128, 1024], P(('dp', 'fsdp'), None, 'row')
- grad_w_out: float32 [1024, 2048], P(('fsdp', 'row'))
- grad_w_val: float32 [2048, 1024], P(('fsdp', 'row'))
All inputs are finite; a program needn't handle non-finite values.
Results may differ from a plain program's by a relative error of at most 0.014.
Values may be sent and summed in bfloat16 or wider, within the bound.
A program may use at most 192 MiB of HBM per device.

v0:
```python
import math

import jax
import jax.numpy as jnp
from jax import lax
from jax.sharding import PartitionSpec as P

HD = 128


def split_heads(values):
    return values.reshape(values.shape[:2] + (-1, HD))


def probabilities(queries, key_block, layout):
    key_layout = layout.replace("l", "m")
    scores = jnp.einsum(
        layout + "," + key_layout + "->bhlm",
        split_heads(queries),
        split_heads(key_block),
        preferred_element_type=jnp.float32,
    ) / math.sqrt(HD)
    length = queries.shape[layout.index("l")]
    causal = lax.broadcasted_iota(jnp.int32, (length, length), 0) >= lax.broadcasted_iota(
        jnp.int32, (length, length), 1
    )
    scores = jnp.where(causal, scores, -jnp.inf)
    highest = jnp.max(scores, axis=-1, keepdims=True)
    raised = jnp.exp(scores - highest)
    return raised / jnp.sum(raised, axis=-1, keepdims=True)


def weighted(probs_all, values, layout):
    key_layout = layout.replace("l", "m")
    result = jnp.einsum(
        "bhlm," + key_layout + "->" + layout,
        probs_all.astype(jnp.bfloat16),
        split_heads(values),
        preferred_element_type=jnp.float32,
    )
    return result.reshape(values.shape)


def backprop(queries, key_block, values, probs_all, upstream, layout):
    key_layout = layout.replace("l", "m")
    grad_probs = jnp.einsum(
        layout + "," + key_layout + "->bhlm",
        split_heads(upstream),
        split_heads(values),
        preferred_element_type=jnp.float32,
    )
    inner = jnp.sum(probs_all * grad_probs, axis=-1, keepdims=True)
    grad_scores = (probs_all * (grad_probs - inner) / math.sqrt(HD)).astype(jnp.bfloat16)
    grad_queries = jnp.einsum(
        "bhlm," + key_layout + "->" + layout,
        grad_scores,
        split_heads(key_block),
        preferred_element_type=jnp.float32,
    )
    grad_keys = jnp.einsum(
        "bhlm," + layout + "->" + key_layout,
        grad_scores,
        split_heads(queries),
        preferred_element_type=jnp.float32,
    )
    grad_values = jnp.einsum(
        "bhlm," + layout + "->" + key_layout,
        probs_all.astype(jnp.bfloat16),
        split_heads(upstream),
        preferred_element_type=jnp.float32,
    )
    return (
        grad_queries.reshape(queries.shape),
        grad_keys.reshape(queries.shape),
        grad_values.reshape(queries.shape),
    )


def normalize(residual, gain):
    stream = residual.astype(jnp.float32)
    inverse = lax.rsqrt(jnp.mean(stream * stream, axis=-1, keepdims=True) + 1e-05)
    return ((stream * inverse * gain.astype(jnp.float32)).astype(jnp.bfloat16), inverse)


def norm_backward(residual, inverse, gain, grad_normed):
    stream = residual.astype(jnp.float32)
    scaled = grad_normed * gain.astype(jnp.float32)
    cubed = inverse * inverse * inverse
    result = inverse * scaled - stream * cubed * jnp.mean(stream * scaled, axis=-1, keepdims=True)
    return result.astype(jnp.bfloat16)


def outer_sum(left_side, right_side):
    return lax.dot_general(
        left_side, right_side, (((0,), (0,)), ((), ())), preferred_element_type=jnp.float32
    )


def body(patches, q_rows, k_rows, v_rows, w_out, gain, w_val, q_cols, k_cols, cotangent):
    whole_out, whole_val = (
        lax.all_gather(w_out, ("fsdp", "row"), axis=0, tiled=True),
        lax.all_gather(w_val, ("fsdp", "row"), axis=0, tiled=True),
    )
    rows_dev = patches.shape[1]
    columns = patches.shape[2]
    features = patches.shape[3]
    inner_width = q_rows.shape[3]
    probs_rows = probabilities(q_rows[0], k_rows[0], "blhd")
    attended = weighted(probs_rows, v_rows[0], "blhd").astype(jnp.bfloat16)
    att_rows = attended.reshape(-1, inner_width)
    residual = (
        patches.reshape(-1, features).astype(jnp.float32)
        + jnp.dot(att_rows, whole_out, preferred_element_type=jnp.float32)
    ).astype(jnp.bfloat16)
    exchanged = lax.all_to_all(
        residual.reshape(1, rows_dev, columns, features),
        "row",
        split_axis=2,
        concat_axis=1,
        tiled=True,
    )
    stream_col = exchanged.reshape(-1, features)
    normed, inverse = normalize(stream_col, gain)
    values = (
        jnp.dot(normed, whole_val, preferred_element_type=jnp.float32)
        .astype(jnp.bfloat16)
        .reshape(q_cols.shape[1:])
    )
    probs_cols = probabilities(q_cols[0], k_cols[0], "lbhd")
    grad_qcol, grad_kcol, grad_vcol = backprop(
        q_cols[0], k_cols[0], values, probs_cols, cotangent[0], "lbhd"
    )
    grad_values = grad_vcol.astype(jnp.bfloat16).reshape(-1, inner_width)
    grad_normed = jnp.dot(grad_values, whole_val.T, preferred_element_type=jnp.float32)
    grad_col = norm_backward(stream_col, inverse, gain, grad_normed).reshape(exchanged.shape)
    grad_stream = lax.all_to_all(grad_col, "row", split_axis=1, concat_axis=2, tiled=True).reshape(
        -1, features
    )
    grad_att = (
        jnp.dot(grad_stream, whole_out.T, preferred_element_type=jnp.float32)
        .astype(jnp.bfloat16)
        .reshape(q_rows.shape[1:])
    )
    grad_qrow, grad_krow, grad_vrow = backprop(
        q_rows[0], k_rows[0], v_rows[0], probs_rows, grad_att, "blhd"
    )
    grad_wout = lax.psum_scatter(
        outer_sum(att_rows, grad_stream), ("fsdp", "row"), scatter_dimension=0, tiled=True
    )
    grad_wval = lax.psum_scatter(
        outer_sum(normed, grad_values), ("fsdp", "row"), scatter_dimension=0, tiled=True
    )
    grad_wout, grad_wval = (
        lax.psum(grad_wout.astype(jnp.bfloat16), "dp").astype(jnp.float32),
        lax.psum(grad_wval.astype(jnp.bfloat16), "dp").astype(jnp.float32),
    )
    return (
        grad_stream.reshape(patches.shape),
        grad_qrow.astype(jnp.bfloat16).reshape(q_rows.shape),
        grad_krow.astype(jnp.bfloat16).reshape(q_rows.shape),
        grad_vrow.astype(jnp.bfloat16).reshape(q_rows.shape),
        grad_qcol.astype(jnp.bfloat16).reshape(q_cols.shape),
        grad_kcol.astype(jnp.bfloat16).reshape(q_cols.shape),
        grad_wout,
        grad_wval,
    )


def solution(mesh):
    placed = (
        P(("dp", "fsdp"), "row", None, None),
        P(("dp", "fsdp"), "row", None, None),
        P(("dp", "fsdp"), "row", None, None),
        P(("dp", "fsdp"), "row", None, None),
        P(("fsdp", "row"), None),
        P(),
        P(("fsdp", "row"), None),
        P(("dp", "fsdp"), None, "row", None),
        P(("dp", "fsdp"), None, "row", None),
        P(("dp", "fsdp"), None, "row", None),
    )
    return jax.shard_map(
        body,
        mesh=mesh,
        in_specs=placed,
        out_specs=(
            P(("dp", "fsdp"), "row", None, None),
            P(("dp", "fsdp"), "row", None, None),
            P(("dp", "fsdp"), "row", None, None),
            P(("dp", "fsdp"), "row", None, None),
            P(("dp", "fsdp"), None, "row", None),
            P(("dp", "fsdp"), None, "row", None),
            P(("fsdp", "row"), None),
            P(("fsdp", "row"), None),
        ),
        check_vma=False,
    )
```

profile of v0, /device:TPU:1, one launch (start us, length us, event | category | flops | bytes accessed | tf_op | source)
XLA Modules:
  0.0 848.3 jit_solution(2294593596858269043)
XLA Ops:
  10.0 1.5 copy.202
  14.2 116.2 %all-gather.3.cloned.1.call-done = bf16[1024,2048]{1,0:T(8,128)(2,1)} async-done(((bf16[16,2048]{1,0:T(8,128)(2,1)}), bf16[1024,2048]{1,0:T(8,128)(2,1)}) %all-gather.3.cloned.1.call-update) | async-done | bytes 4194320 | tf_op jit(solution)/shard_map/all_gather | solution.py:101
  130.4 3.7 fusion.4
  134.2 2.0 copy.169
  136.2 3.7 all-to-all-start
  140.2 2.3 fusion.25
  143.7 1.6 fusion.31
  146.6 11.5 %all-to-all-done = bf16[1,2,128,2048]{3,1,0,2:T(2,128)(2,1)S(1)} async-done(((bf16[1,2,128,2048]{3,1,0,2:T(2,128)(2,1)}), bf16[1,2,128,2048]{3,1,0,2:T(2,128)(2,1)S(1)}, u32[]{:S(2)}, u32[]{:S(2)}) %all-to-all-start) | async-done | bytes 1048608 | tf_op jit(solution)/shard_map/all_to_all | solution.py:115
  160.5 2.0 fusion.13
  162.4 4.5 fusion.43
  167.0 1.6 copy.170
  168.8 81.6 %all-gather.5.cloned.1.call-done = bf16[2048,1024]{1,0:T(8,128)(2,1)} async-done(((bf16[32,1024]{1,0:T(8,128)(2,1)}), bf16[2048,1024]{1,0:T(8,128)(2,1)}) %all-gather.5.cloned.1.call-update) | async-done | bytes 4194320 | tf_op jit(solution)/shard_map/all_gather | solution.py:102
  250.4 3.6 fusion.8
  254.0 1.6 fusion.10
  255.6 24.9 %all_to_all.27 = bf16[1,32,8,2048]{3,2,0,1:T(8,128)(2,1)S(1)} all-to-all(bf16[1,32,8,2048]{3,2,0,1:T(8,128)(2,1)S(1)} %bitcast.125), channel_id=1, replica_groups=mesh['dp'=4,'fsdp'=4,'row'=16] {'row'}, dimensions={1} | all-to-all | bytes 2097152 | tf_op jit(solution)/shard_map/all_to_all | solution.py:136
  280.7 4.5 fusion.46
  286.4 3.4 fusion.29
  289.9 2.2 convolution_bitcast_fusion
  292.1 3.2 fusion.33
  297.6 2.6 fusion.32
  301.4 3.5 fusion.28
  306.3 2.9 convolution_convert_fusion.4
  309.2 2.0 copy.194
  311.3 2.0 convolution_convert_fusion
  314.3 205.3 %reduce-scatter.5.cloned.1.call-done = f32[32,1024]{1,0:T(8,128)} async-done(((f32[2048,1024]{1,0:T(8,128)}), f32[32,1024]{1,0:T(8,128)}) %reduce-scatter.5.cloned.1.call-update) | async-done | bytes 131088 | tf_op jit(solution)/shard_map/reduce_scatter | solution.py:150
  519.6 1.5 convert_element_type.220
  521.1 269.4 %reduce-scatter.3.cloned.1.call-done = f32[16,2048]{1,0:T(8,128)} async-done(((f32[1024,2048]{1,0:T(8,128)}), f32[16,2048]{1,0:T(8,128)}) %reduce-scatter.3.cloned.1.call-update) | async-done | bytes 131088 | tf_op jit(solution)/shard_map/reduce_scatter | solution.py:147
  790.5 1.5 convert_element_type.216
  792.1 2.2 convolution_convert_fusion.3
  795.3 43.5 %all-reduce.3.cloned.1.call-done = (bf16[16,2048]{1,0:T(8,128)(2,1)}, bf16[32,1024]{1,0:T(8,128)(2,1)}) async-done(((bf16[16,2048]{1,0:T(8,128)(2,1)}, bf16[32,1024]{1,0:T(8,128)(2,1)}), (bf16[16,2048]{1,0:T(8,128)(2,1)}, bf16[32,1024]{1,0:T(8,128)(2,1)})) %all-reduce.3.cloned.1.call-update) | async-done | bytes 131088 | tf_op jit(solution)/shard_map/psum | solution.py:154
  838.8 1.5 convert_element_type.217
  840.3 1.5 convert_element_type.221
  (73 shorter events, 18.7 us)
Async XLA Ops:
  7.2 136.6 %copy-start = (bf16[1,32,8,1024]{3,2,1,0:T(8,128)(2,1)S(1)}, bf16[1,32,8,1024]{3,2,1,0:T(8,128)(2,1)}, u32[]{:S(2)}) copy-start(bf16[1,32,8,1024]{3,2,1,0:T(8,128)(2,1)} %param.19) | copy-start | bytes 1572868
  7.2 4.3 copy-start.14
  7.2 123.2 %all-gather.3.cloned.1.call-start = ((), (), s32[]{:S(2)}) async-start(), calls=%async_computation.4 | async-start | bytes 4259840 | tf_op jit(solution)/shard_map/all_gather | solution.py:101
  7.9 242.5 %all-gather.5.cloned.1.call-start = ((), (), s32[]{:S(2)}) async-start(), calls=%async_computation.5 | async-start | bytes 4259840 | tf_op jit(solution)/shard_map/all_gather | solution.py:102
  10.0 2.0 copy-start.8
  11.5 1.8 copy-start.6
  11.6 1.7 copy-start.10
  12.0 1.8 copy-start.3
  14.2 119.9 %copy-start.4 = (bf16[2,128,8,128]{3,2,1,0:T(8,128)(2,1)}, bf16[2,128,8,128]{3,2,1,0:T(8,128)(2,1)S(1)}, u32[]{:S(2)}) copy-start(bf16[2,128,8,128]{3,2,1,0:T(8,128)(2,1)S(1)} %copy.168) | copy-start | bytes 1572868
  134.1 6.0 copy-start.15
  134.1 6.0 copy-start.16
  136.2 21.9 %all-to-all-start = ((bf16[1,2,128,2048]{3,1,0,2:T(2,128)(2,1)}), bf16[1,2,128,2048]{3,1,0,2:T(2,128)(2,1)S(1)}, u32[]{:S(2)}, u32[]{:S(2)}) async-start(bf16[1,2,128,2048]{3,1,0,2:T(2,128)(2,1)} %copy.169), calls=%async_computation | async-start | bytes 2097152 | tf_op jit(solution)/shard_map/all_to_all | solution.py:115
  139.9 379.7 %reduce-scatter.5.cloned.1.call-start = ((), (), s32[]{:S(2)}) async-start(), calls=%async_computation.7 | async-start | bytes 8519680 | tf_op jit(solution)/shard_map/reduce_scatter | solution.py:150
  158.1 2.3 copy-start.1
  167.0 623.5 %reduce-scatter.3.cloned.1.call-start = ((), (), s32[]{:S(2)}) async-start(), calls=%async_computation.6 | async-start | bytes 8519680 | tf_op jit(solution)/shard_map/reduce_scatter | solution.py:147
  255.6 25.0 %copy-start.5 = (bf16[2,128,8,128]{3,2,1,0:T(8,128)(2,1)S(1)}, bf16[2,128,8,128]{3,2,1,0:T(8,128)(2,1)}, u32[]{:S(2)}) copy-start(bf16[2,128,8,128]{3,2,1,0:T(8,128)(2,1)} %copy-done.4) | copy-start | bytes 1572868
  280.7 20.8 %copy-start.2 = (bf16[1,2,16,8,2048]{4,3,2,1,0:T(8,128)(2,1)}, bf16[1,2,16,8,2048]{4,3,2,1,0:T(8,128)(2,1)S(1)}, u32[]{:S(2)}) copy-start(bf16[1,2,16,8,2048]{4,3,2,1,0:T(8,128)(2,1)S(1)} %copy.249) | copy-start | bytes 3145732
  285.2 1.2 copy-start.12
  285.2 553.6 %all-reduce.3.cloned.1.call-start = ((), (), s32[]{:S(2)}) async-start(), calls=%async_computation.8 | async-start | bytes 262144 | tf_op jit(solution)/shard_map/psum | solution.py:154
  289.9 2.2 copy-start.13
  289.9 2.2 copy-start.17
  304.9 1.0 copy-start.11
  304.9 1.3 copy-start.9
  306.3 5.0 copy-start.7
Sparse Core Ops, SparseCore 0:
  9.9 120.4 all-gather.2
  132.2 118.1 all-gather.4
  253.0 266.5 reduce-scatter.4
  522.0 268.5 reduce-scatter.2
  793.3 45.3 all-reduce.2
where the time goes:
time: 850 us; the launch traced here: 848 us
  waiting for transfers between devices  729 us (86%)
  matrix products  43.5 us (5%)
  blocking collectives  24.9 us (3%)
  local copies, waits for them, and re-layouts  18.2 us (2%)
  other arithmetic  14.6 us (2%)
  between operations  14.1 us (2%)
    reduce_scatter x1, waiting for transfers between devices, body(): lax.psum_scatter(outer_sum(att_rows, grad_stream), ('fsdp', 'row'), scatt...  269 us
    reduce_scatter x1, waiting for transfers between devices, body(): lax.psum_scatter(outer_sum(normed, grad_values), ('fsdp', 'row'), scatter...  205 us
    all_gather x1, waiting for transfers between devices, body(): lax.all_gather(w_out, ('fsdp', 'row'), axis=0, tiled=True)  116 us
    all_gather x1, waiting for transfers between devices, body(): lax.all_gather(w_val, ('fsdp', 'row'), axis=0, tiled=True)  81.6 us
    psum x1, waiting for transfers between devices, body(): lax.psum(grad_wout.astype(jnp.bfloat16), 'dp').astype(jnp.float32)  43.5 us
    all_to_all x1, blocking collectives, body(): lax.all_to_all(grad_col, 'row', split_axis=1, concat_axis=2, tiled=True)  24.9 us
  transfers between devices with their start and end apart: 6, of which 6 were waited for; matrix products, arithmetic and copies ran while one was open for 8% of the time, Pallas kernels for 0%

commit v1 on v0

v1 whole, which is shorter than its diff:
```python
import functools
import math

import jax
import jax.numpy as jnp
from jax import lax
from jax.experimental import pallas as pl
from jax.experimental.pallas import tpu as pltpu
from jax.sharding import PartitionSpec as P

HD = 128
HEADS = 8
D = 2048
HW = 1024
T = 256
COPIES = 256
SCALE = 1.0 / math.sqrt(HD)
MESH = pl.DeviceIdType.MESH
F32 = jnp.float32
BF16 = jnp.bfloat16


def dot(a, b, da, db):
    return lax.dot_general(a, b, (((da,), (db,)), ((), ())), preferred_element_type=F32)


def softmax(scores, keep):
    scores = jnp.where(keep, scores * SCALE, -jnp.inf)
    raised = jnp.exp(scores - jnp.max(scores, axis=-1, keepdims=True))
    return raised * (1.0 / jnp.sum(raised, axis=-1, keepdims=True))


def kernel(
    patches, q_rows, k_rows, v_rows, w_out, gain, w_val, q_cols, k_cols, cotangent,
    g_patches, g_qrow, g_krow, g_vrow, g_qcol, g_kcol, g_wout, g_wval,
    Wo, Wv, p_rows, p_cols, att2, gv_col, gv_in, gv_row, gv2, resid, inverse, normed2, scaled,
    val_out, val_in, gp2, g_att,
    Go, Gv, to, tv, so, sv, uo, uv, zo, zv, fo, fv, oo, ov,
    send_sems, recv_sems, local_sems,
):
    x, f, r = lax.axis_index("dp"), lax.axis_index("fsdp"), lax.axis_index("row")
    y, zl, c = r // 4, (r // 2) % 2, r % 2
    z = f * 2 + zl

    def place(px, py, pz, pc):
        return {"dp": px, "fsdp": pz // 2, "row": py * 4 + (pz % 2) * 2 + pc}

    def at_x(k):
        return place((x + k) % 4, y, z, c)

    def at_y(k):
        return place(x, (y + k) % 4, z, c)

    def at_z(k):
        return place(x, y, (z + k) % 8, c)

    def at_row(k):
        return {"dp": x, "fsdp": f, "row": (r + k) % 16}

    sibling = place(x, y, z, 1 - c)

    barrier = pltpu.get_barrier_semaphore()
    peers = [at_row(k) for k in range(1, 16)]
    peers += [place(x, y, ((f + k) % 4) * 2 + s, c) for k in range(1, 4) for s in range(2)]
    peers += [place((x + k) % 4, y, z, s) for k in range(1, 4) for s in range(2)]
    for peer in peers:
        pl.semaphore_signal(barrier, inc=1, device_id=peer, device_id_type=MESH)
    pl.semaphore_wait(barrier, len(peers))

    used = [0]
    sent = []

    def slots(n):
        first = used[0]
        used[0] += n
        assert used[0] <= COPIES
        return first

    def remote(src, dst, where, i):
        return pltpu.make_async_remote_copy(
            src_ref=src, dst_ref=dst, send_sem=send_sems.at[i], recv_sem=recv_sems.at[i],
            device_id=where, device_id_type=MESH,
        )

    def send(src, dst, where, i):
        copy = remote(src, dst, where, i)
        copy.start()
        sent.append(copy)

    def arrived(region, i):
        remote(region, region, sibling, i).wait_recv()

    class Gather:
        def __init__(self, W, own, cols, local):
            self.W, self.own, self.q = W, own, cols // 4
            self.local = local
            self.z, self.two, self.one, self.sib = slots(7), slots(6), slots(12), slots(16)

        def quarter(self, k):
            return pl.ds(pl.multiple_of(((x + k) % 4) * self.q, 128), self.q)

        def start_z(self):
            mine = self.own.at[:, self.quarter(0)]
            there = self.W.at[f, y, zl, c, :, self.quarter(0)]
            self.keep = pltpu.make_async_copy(mine, there, local_sems.at[self.local])
            self.keep.start()
            for k in range(1, 8):
                send(mine, there, at_z(k), self.z + k - 1)

        def start_two(self):
            self.keep.wait()
            for k in range(1, 8):
                pz = (z + 8 - k) % 8
                arrived(self.W.at[pz // 2, y, pz % 2, c, :, self.quarter(0)], self.z + k - 1)
            for part in range(2):
                block = self.W.at[pl.ds(2 * part, 2), y, :, c, :, self.quarter(0)]
                for k in range(1, 4):
                    send(block, block, (at_x if part == 0 else at_y)(k), self.two + 3 * part + k - 1)

        def chunk(self, part, j, k):
            if part == 0:
                return self.W.at[j, (y + k) % 4, :, c, :, :]
            return self.W.at[2 + j, :, :, c, :, self.quarter(k)]

        def other(self, part, j, k):
            if part == 0:
                return self.W.at[j, (y + k) % 4, :, 1 - c, :, :]
            return self.W.at[2 + j, :, :, 1 - c, :, self.quarter(k)]

        def share(self, part, j, k, i):
            block = self.chunk(part, j, k)
            send(block, block, sibling, self.sib + 8 * part + i)

        def start_one(self):
            for part in range(2):
                for k in range(1, 4):
                    if part == 0:
                        region = self.W.at[pl.ds(0, 2), y, :, c, :, self.quarter(4 - k)]
                    else:
                        region = self.W.at[pl.ds(2, 2), (y + 4 - k) % 4, :, c, :, self.quarter(0)]
                    arrived(region, self.two + 3 * part + k - 1)
            for part in range(2):
                at = at_y if part == 0 else at_x
                first = self.one + 6 * part
                a, b = self.chunk(part, 0, 0), self.chunk(part, 1, 0)
                send(a, a, at(1), first)
                send(b, b, at(3), first + 1)
                send(b, b, at(1), first + 2)
                send(a, a, at(3), first + 3)
            for part in range(2):
                self.share(part, 0, 0, 0)
                self.share(part, 1, 0, 1)

        def forward(self):
            for part in range(2):
                at = at_y if part == 0 else at_x
                first = self.one + 6 * part
                a, b = self.chunk(part, 0, 3), self.chunk(part, 1, 1)
                arrived(a, first)
                send(a, a, at(1), first + 4)
                self.share(part, 0, 3, 2)
                arrived(b, first + 1)
                send(b, b, at(3), first + 5)
                self.share(part, 1, 1, 3)

        def nearer(self):
            for part in range(2):
                first = self.one + 6 * part
                arrived(self.chunk(part, 1, 3), first + 2)
                self.share(part, 1, 3, 4)
                arrived(self.chunk(part, 0, 1), first + 3)
                self.share(part, 0, 1, 5)

        def farther(self):
            for part in range(2):
                first = self.one + 6 * part
                arrived(self.chunk(part, 0, 2), first + 4)
                self.share(part, 0, 2, 6)
                arrived(self.chunk(part, 1, 2), first + 5)
                self.share(part, 1, 2, 7)

        def finish(self):
            order = ((0, 0), (1, 0), (0, 3), (1, 1), (1, 3), (0, 1), (0, 2), (1, 2))
            for part in range(2):
                for i, (j, k) in enumerate(order):
                    arrived(self.other(part, j, k), self.sib + 8 * part + i)

    class Scatter:
        def __init__(self, G, t, s, u, zb, fin, o, out, rows, cols, local):
            self.G, self.t, self.s, self.u, self.zb, self.fin, self.o = G, t, s, u, zb, fin, o
            self.out, self.rows, self.q, self.local = out, rows, cols // 8, local
            self.one, self.two, self.three, self.four = slots(12), slots(6), slots(7), slots(7)

        def quarter(self, k):
            return pl.ds(pl.multiple_of(((x + k) % 4) * self.q, 128), self.q)

        def chunk(self, part, j, k):
            if part == 0:
                return self.G.at[j, (y + k) % 4, :, :, :, :]
            return self.G.at[2 + j, :, :, :, :, self.quarter(k)]

        def start_one(self, part):
            at = at_y if part == 0 else at_x
            first = self.one + 6 * part
            t, s = self.t[part], self.s[part]
            send(self.chunk(part, 0, 2), t.at[0], at(1), first)
            send(self.chunk(part, 1, 2), t.at[1], at(3), first + 1)
            send(self.chunk(part, 1, 1), s.at[0, 1], at(1), first + 2)
            send(self.chunk(part, 0, 3), s.at[1, 0], at(3), first + 3)

        def add_into(self, target, others):
            for lead in range(target.shape[0]):
                total = target[lead].astype(F32)
                for other in others:
                    total = total + other[lead].astype(F32)
                target[lead] = total.astype(BF16)

        def merge(self, part):
            at = at_y if part == 0 else at_x
            first = self.one + 6 * part
            t, s = self.t[part], self.s[part]
            arrived(t.at[0], first)
            self.add_into(self.chunk(part, 0, 1), [t.at[0]])
            send(self.chunk(part, 0, 1), s.at[0, 0], at(1), first + 4)
            arrived(t.at[1], first + 1)
            self.add_into(self.chunk(part, 1, 3), [t.at[1]])
            send(self.chunk(part, 1, 3), s.at[1, 1], at(3), first + 5)

        def piece(self, part, k):
            if part == 0:
                return self.G.at[pl.ds(0, 2), y, :, :, :, self.quarter(k)]
            return self.G.at[pl.ds(2, 2), (y + k) % 4, :, :, :, self.quarter(0)]

        def start_two(self, part):
            first = self.one + 6 * part
            s = self.s[part]
            arrived(s.at[0, 1], first + 2)
            arrived(s.at[1, 1], first + 5)
            self.add_into(self.chunk(part, 1, 0), [s.at[0, 1], s.at[1, 1]])
            arrived(s.at[1, 0], first + 3)
            arrived(s.at[0, 0], first + 4)
            self.add_into(self.chunk(part, 0, 0), [s.at[0, 0], s.at[1, 0]])
            for k in range(1, 4):
                send(
                    self.piece(part, k), self.u.at[part, k - 1],
                    (at_x if part == 0 else at_y)(k), self.two + 3 * part + k - 1,
                )

        def end_two(self, part):
            for k in range(1, 4):
                arrived(self.u.at[part, k - 1], self.two + 3 * part + k - 1)
            self.add_into(self.piece(part, 0), [self.u.at[part, k] for k in range(3)])

        def start_three(self):
            for k in range(1, 8):
                pz = (z + k) % 8
                send(
                    self.G.at[pz // 2, y, pz % 2, :, :, self.quarter(0)], self.zb.at[k - 1],
                    at_z(k), self.three + k - 1,
                )

        def start_four(self):
            for k in range(1, 8):
                arrived(self.zb.at[k - 1], self.three + k - 1)
            for pc in range(2):
                total = self.G[f, y, zl, pc, :, self.quarter(0)].astype(F32)
                for k in range(7):
                    total = total + self.zb[k, pc].astype(F32)
                self.fin[pc] = total
            self.keep = pltpu.make_async_copy(
                self.fin.at[c], self.o.at[c, x], local_sems.at[self.local]
            )
            self.keep.start()
            for k in range(4):
                for s in range(2):
                    if k or s:
                        pc = (c + s) % 2
                        send(
                            self.fin.at[pc], self.o.at[c, x], place((x + k) % 4, y, z, pc),
                            self.four + 2 * k + s - 1,
                        )

        def finish(self):
            self.keep.wait()
            for k in range(4):
                for s in range(2):
                    if k or s:
                        arrived(
                            self.o.at[(c + s) % 2, (x + 4 - k) % 4], self.four + 2 * k + s - 1
                        )
            for pc in range(2):
                for px in range(4):
                    first = (4 * pc + px) * self.q
                    self.out[:, first : first + self.q] = self.o[pc, px]

    gather_o = Gather(Wo, w_out, D, 0)
    gather_v = Gather(Wv, w_val, HW, 1)
    scatter_o = Scatter(Go, to, so, uo, zo, fo, oo, g_wout, 16, D, 2)
    scatter_v = Scatter(Gv, tv, sv, uv, zv, fv, ov, g_wval, 32, HW, 3)
    s_gv, s_val, s_act = slots(15), slots(15), slots(4)

    def head(h):
        return pl.ds(pl.multiple_of(h * HD, HD), HD)

    row_keep = lax.broadcasted_iota(jnp.int32, (128, 128), 0) >= lax.broadcasted_iota(
        jnp.int32, (128, 128), 1
    )

    def row_forward(i, _):
        rows, cols = pl.ds(pl.multiple_of((i // HEADS) * 128, 128), 128), head(i % HEADS)
        probs = softmax(dot(q_rows[rows, cols], k_rows[rows, cols], 1, 1), row_keep)
        p_rows[i] = probs
        att2[c, rows, cols] = dot(probs.astype(BF16), v_rows[rows, cols], 1, 0).astype(BF16)
        return 0

    def row_backward(i, _):
        rows, cols = pl.ds(pl.multiple_of((i // HEADS) * 128, 128), 128), head(i % HEADS)
        probs, upstream = p_rows[i], g_att[rows, cols]
        grad = dot(upstream, v_rows[rows, cols], 1, 1)
        inner = jnp.sum(probs * grad, axis=-1, keepdims=True)
        ds = (probs * (grad - inner) * SCALE).astype(BF16)
        g_qrow[rows, cols] = dot(ds, k_rows[rows, cols], 1, 0).astype(BF16)
        g_krow[rows, cols] = dot(ds, q_rows[rows, cols], 0, 0).astype(BF16)
        g_vrow[rows, cols] = dot(probs.astype(BF16), upstream, 0, 0).astype(BF16)
        return 0

    def col_forward(h, _):
        cols = head(h)
        i = lax.broadcasted_iota(jnp.int32, (T, T), 0)
        j = lax.broadcasted_iota(jnp.int32, (T, T), 1)
        keep = (i >= j) & ((i - j) % 8 == 0)
        probs = softmax(dot(q_cols[:, cols], k_cols[:, cols], 1, 1), keep)
        p_cols[h] = probs
        gv_col[:, cols] = dot(probs.astype(BF16), cotangent[:, cols], 0, 0).astype(BF16)
        return 0

    def col_backward(h, _):
        cols = head(h)
        probs = p_cols[h]
        grad = dot(cotangent[:, cols], val_in[:, cols], 1, 1)
        inner = jnp.sum(probs * grad, axis=-1, keepdims=True)
        ds = (probs * (grad - inner) * SCALE).astype(BF16)
        g_qcol[:, cols] = dot(ds, k_cols[:, cols], 1, 0).astype(BF16)
        g_kcol[:, cols] = dot(ds, q_cols[:, cols], 0, 0).astype(BF16)
        return 0

    def block(ref, k):
        return ref.at[pl.ds(pl.multiple_of(((r + k) % 16) * 16, 16), 16)]

    gather_o.start_z()
    gather_v.start_z()
    lax.fori_loop(0, 4, col_forward, 0)
    gather_o.start_two()
    gather_v.start_two()
    lax.fori_loop(4, 8, col_forward, 0)
    for k in range(1, 16):
        send(block(gv_col, k), block(gv_in, 0), at_row(k), s_gv + k - 1)
    keep_gv = pltpu.make_async_copy(block(gv_col, 0), block(gv_in, 0), local_sems.at[4])
    keep_gv.start()
    gather_o.start_one()
    lax.fori_loop(0, 8, row_forward, 0)
    gather_o.forward()
    gather_v.start_one()
    lax.fori_loop(8, 16, row_forward, 0)
    send(att2.at[c], att2.at[c], sibling, s_act)
    gather_o.nearer()

    keep_gv.wait()
    for k in range(1, 16):
        arrived(block(gv_in, 16 - k), s_gv + k - 1)
    for piece in range(0, HW, 256):
        cols = slice(piece, piece + 256)
        moved = gv_in[:, cols].astype(F32).reshape(16, 2, 8, 256)
        for s in range(2):
            gv_row[128 * s : 128 * s + 128, cols] = moved[:, s].reshape(128, 256).astype(BF16)

    def half(k, n):
        return pl.ds(pl.multiple_of(((c + k) % 2) * n, 128), n)

    send(gv_row.at[:, half(1, HW // 2)], gv2.at[c], sibling, s_act + 1)
    gv2[c] = gv_row[:, half(0, HW // 2)]

    gather_o.farther()
    gather_o.finish()

    def residual_tile(i, _):
        cols = pl.ds(pl.multiple_of(i * 512, 512), 512)
        weight = Wo[:, :, :, :, :, cols].reshape(HW, 512)
        resid[:, cols] = (dot(att2[c], weight, 1, 0) + patches[:, cols].astype(F32)).astype(BF16)
        return 0

    lax.fori_loop(0, D // 512, residual_tile, 0)
    gather_v.forward()

    def norm_rows(i, _):
        rows = pl.ds(pl.multiple_of(i * 16, 16), 16)
        stream = resid[rows, :].astype(F32)
        inv = lax.rsqrt(jnp.mean(stream * stream, axis=-1, keepdims=True) + 1e-05)
        inverse[rows, :] = jnp.broadcast_to(inv, (16, 128))
        normed2[c, rows, :] = (stream * inv * gain[...].astype(F32)).astype(BF16)
        return 0

    lax.fori_loop(0, T // 16, norm_rows, 0)
    send(normed2.at[c], normed2.at[c], sibling, s_act + 2)
    gather_v.nearer()
    arrived(gv2.at[1 - c], s_act + 1)
    arrived(normed2.at[1 - c], s_act + 2)

    def wval_tile(i, _):
        left = normed2[:, :, pl.ds(pl.multiple_of(i * 512, 512), 512)].reshape(2 * T, 512)
        Gv[i] = dot(left, gv2[...].reshape(2 * T, 512), 0, 0).astype(BF16).reshape(4, 2, 2, 32, 512)
        return 0

    lax.fori_loop(0, 2, wval_tile, 0)
    scatter_v.start_one(0)
    lax.fori_loop(2, 4, wval_tile, 0)
    scatter_v.start_one(1)
    gather_v.farther()
    gather_v.finish()

    scaled_sum = jnp.zeros((T, 128), F32)

    def normed_grad_tile(i, total):
        cols = pl.ds(pl.multiple_of(i * 512, 512), 512)
        weight = Wv[i].reshape(512, HW)
        grad = dot(gv_row[...], weight, 1, 1) * gain[:, cols].astype(F32)
        scaled[:, cols] = grad
        product = grad * resid[:, cols].astype(F32)
        return total + sum(product[:, 128 * k : 128 * k + 128] for k in range(4))

    scaled_sum = lax.fori_loop(0, 4, normed_grad_tile, scaled_sum)
    scaled[:, D:] = scaled_sum

    def stream_rows(i, _):
        rows = pl.ds(pl.multiple_of(i * 16, 16), 16)
        inv = inverse[rows, 0:1]
        mean = jnp.sum(scaled[rows, D:], axis=-1, keepdims=True) * (1.0 / D)
        stream = resid[rows, :].astype(F32)
        result = inv * scaled[rows, :D] - stream * (inv * inv * inv * mean)
        g_patches[rows, :] = result.astype(BF16)
        return 0

    lax.fori_loop(0, T // 16, stream_rows, 0)
    send(g_patches.at[:, half(1, D // 2)], gp2.at[c], sibling, s_act + 3)
    gp2[c] = g_patches[:, half(0, D // 2)]
    scatter_v.merge(0)
    scatter_v.merge(1)
    arrived(att2.at[1 - c], s_act)
    arrived(gp2.at[1 - c], s_act + 3)

    def wout_tile(i, _):
        left = att2[:, :, pl.ds(pl.multiple_of(i * 256, 256), 256)].reshape(2 * T, 256)
        Go[i] = dot(left, gp2[...].reshape(2 * T, HW), 0, 0).astype(BF16).reshape(4, 2, 2, 16, HW)
        return 0

    lax.fori_loop(0, 2, wout_tile, 0)
    scatter_o.start_one(0)
    lax.fori_loop(2, 4, wout_tile, 0)
    scatter_o.start_one(1)

    def values_tile(i, _):
        cols = pl.ds(pl.multiple_of(i * 256, 256), 256)
        weight = Wv[:, :, :, :, :, cols].reshape(D, 256)
        value = dot(normed2[c], weight, 1, 0).reshape(2, 16, 8, 256)
        both = jnp.concatenate([value[0][:, None], value[1][:, None]], axis=1)
        val_out[:, cols] = both.reshape(T, 256).astype(BF16)
        return 0

    lax.fori_loop(0, HW // 256, values_tile, 0)
    for k in range(1, 16):
        send(block(val_out, k), block(val_in, 0), at_row(k), s_val + k - 1)
    keep_val = pltpu.make_async_copy(block(val_out, 0), block(val_in, 0), local_sems.at[5])
    keep_val.start()

    scatter_v.start_two(0)
    scatter_v.start_two(1)

    def att_grad_tile(i, _):
        weight = Wo[i].reshape(256, D)
        g_att[:, pl.ds(pl.multiple_of(i * 256, 256), 256)] = dot(
            g_patches[...], weight, 1, 1
        ).astype(BF16)
        return 0

    lax.fori_loop(0, 4, att_grad_tile, 0)
    scatter_o.merge(0)
    scatter_o.merge(1)
    lax.fori_loop(0, 8, row_backward, 0)
    scatter_v.end_two(0)
    scatter_v.end_two(1)
    scatter_v.start_three()
    lax.fori_loop(8, 16, row_backward, 0)
    scatter_o.start_two(0)
    scatter_o.start_two(1)
    scatter_v.start_four()
    keep_val.wait()
    for k in range(1, 16):
        arrived(block(val_in, 16 - k), s_val + k - 1)
    lax.fori_loop(0, 4, col_backward, 0)
    scatter_o.end_two(0)
    scatter_o.end_two(1)
    scatter_o.start_three()
    lax.fori_loop(4, 8, col_backward, 0)
    scatter_v.finish()
    scatter_o.start_four()
    scatter_o.finish()
    for copy in sent:
        copy.wait_send()


def body(patches, q_rows, k_rows, v_rows, w_out, gain, w_val, q_cols, k_cols, cotangent):
    vmem = pl.BlockSpec(memory_space=pltpu.VMEM)
    outs = [(T, D), (T, HW), (T, HW), (T, HW), (T, HW), (T, HW)]
    out_shape = [jax.ShapeDtypeStruct(s, BF16) for s in outs]
    out_shape += [jax.ShapeDtypeStruct((16, D), F32), jax.ShapeDtypeStruct((32, HW), F32)]

    def reduce_buffers(rows, cols):
        h, q = cols // 2, cols // 8
        return (
            pltpu.VMEM((4, 4, 2, 2, rows, h), BF16),
            (pltpu.VMEM((2, 2, 2, rows, h), BF16), pltpu.VMEM((2, 4, 2, 2, rows, q), BF16)),
            (pltpu.VMEM((2, 2, 2, 2, rows, h), BF16), pltpu.VMEM((2, 2, 4, 2, 2, rows, q), BF16)),
            pltpu.VMEM((2, 3, 2, 2, 2, rows, q), BF16),
            pltpu.VMEM((7, 2, rows, q), BF16),
            pltpu.VMEM((2, rows, q), F32),
            pltpu.VMEM((2, 4, rows, q), F32),
        )

    ro, rv = reduce_buffers(16, D), reduce_buffers(32, HW)
    scratch = [
        pltpu.VMEM((4, 4, 2, 2, 16, D), BF16),
        pltpu.VMEM((4, 4, 2, 2, 32, HW), BF16),
        pltpu.VMEM((16, 128, 128), F32),
        pltpu.VMEM((HEADS, T, T), F32),
        pltpu.VMEM((2, T, HW), BF16),
        pltpu.VMEM((T, HW), BF16),
        pltpu.VMEM((T, HW), BF16),
        pltpu.VMEM((T, HW), BF16),
        pltpu.VMEM((2, T, HW // 2), BF16),
        pltpu.VMEM((T, D), BF16),
        pltpu.VMEM((T, 128), F32),
        pltpu.VMEM((2, T, D), BF16),
        pltpu.VMEM((T, D + 128), F32),
        pltpu.VMEM((T, HW), BF16),
        pltpu.VMEM((T, HW), BF16),
        pltpu.VMEM((2, T, D // 2), BF16),
        pltpu.VMEM((T, HW), BF16),
    ]
    for a, b in zip(ro, rv):
        scratch += [a, b]
    scratch += [
        pltpu.SemaphoreType.DMA((COPIES,)),
        pltpu.SemaphoreType.DMA((COPIES,)),
        pltpu.SemaphoreType.DMA((6,)),
    ]
    results = pl.pallas_call(
        kernel,
        out_shape=out_shape,
        in_specs=[vmem] * 10,
        out_specs=[vmem] * 8,
        scratch_shapes=scratch,
        compiler_params=pltpu.CompilerParams(
            collective_id=0, has_side_effects=True, vmem_limit_bytes=56 * 2**20
        ),
        name="whole",
    )(
        patches.reshape(T, D), q_rows.reshape(T, HW), k_rows.reshape(T, HW),
        v_rows.reshape(T, HW), w_out, gain.reshape(1, D), w_val, q_cols.reshape(T, HW),
        k_cols.reshape(T, HW), cotangent.reshape(T, HW),
    )
    return (
        results[0].reshape(patches.shape),
        *(results[i].reshape(q_rows.shape) for i in range(1, 4)),
        *(results[i].reshape(q_cols.shape) for i in range(4, 6)),
        results[6],
        results[7],
    )


def solution(mesh):
    rows = P(("dp", "fsdp"), "row", None, None)
    cols = P(("dp", "fsdp"), None, "row", None)
    weights = P(("fsdp", "row"), None)
    return jax.shard_map(
        body,
        mesh=mesh,
        in_specs=(rows, rows, rows, rows, weights, P(), weights, cols, cols, cols),
        out_specs=(rows, rows, rows, rows, cols, cols, weights, weights),
        check_vma=False,
    )
```

time: 850 us -> 115 us (0.14)
  waiting for transfers between devices: 729 us -> 0 us
  Pallas kernels: 0 us -> 103 us
  matrix products: 43.5 us -> 0 us
  blocking collectives: 24.9 us -> 0 us
  other arithmetic: 14.6 us -> 0 us
  between operations: 14.1 us -> 0.67 us
    reduce_scatter x2 -> x0, waiting for transfers between devices: 475 us -> none  [the longest x1 269 us: body(): lax.psum_scatter(outer_sum(att_rows, grad_stream), ('fsdp', 'row'), scatt...]
    all_gather x2 -> x0, waiting for transfers between devices: 198 us -> none  [the longest x1 116 us: body(): lax.all_gather(w_out, ('fsdp', 'row'), axis=0, tiled=True)]
    pallas_call x0 -> x1, Pallas kernels: none -> 103 us  [body(): pl.pallas_call(kernel, out_shape=out_shape, in_specs=[vmem] * 10, out_spe...]
    dot_general x17 -> x0, matrix products: 43.5 us -> none  [the longest x2 9.02 us: outer_sum(): lax.dot_general(left_side, right_side, (((0,), (0,)), ((), ())), preferre...]
    psum x1 -> x0, waiting for transfers between devices: 43.5 us -> none  [body(): lax.psum(grad_wout.astype(jnp.bfloat16), 'dp').astype(jnp.float32)]
    all_to_all x1 -> x0, blocking collectives: 24.9 us -> none  [body(): lax.all_to_all(grad_col, 'row', split_axis=1, concat_axis=2, tiled=True)]
    all_to_all x1 -> x0, waiting for transfers between devices: 11.5 us -> none  [body(): lax.all_to_all(residual.reshape(1, rows_dev, columns, features), 'row', s...]
    convert_element_type x8 -> x0, other arithmetic: 10.8 us -> none  [the longest x2 3.59 us: normalize(): (stream * inverse * gain.astype(jnp.float32)).astype(jnp.bfloat16)]
  transfers between devices with their start and end apart: 6 -> 0, of which waited for: 6 -> 0; matrix products, arithmetic and copies ran while one was open for 8% -> 0% of each run, Pallas kernels for 0% -> 0%
where the time goes in v1:
time: 115 us
  Pallas kernels  103 us (90%)
  local copies, waits for them, and re-layouts  11.2 us (10%)
    pallas_call x1, Pallas kernels, body(): pl.pallas_call(kernel, out_shape=out_shape, in_specs=[vmem] * 10, out_spe...  103 us
    unnamed x24, local copies, waits for them, and re-layouts  10.6 us

profile of v1, /device:TPU:1, one launch (start us, length us, event | category | flops | bytes accessed | tf_op | source)
XLA Modules:
  0.0 115.0 jit_solution(9878923544001023095)
XLA Ops:
  0.6 0.0 copy-start.7
  0.6 0.7 copy-done.7
  1.3 0.6 reshape.62.gain
  1.9 103.1 %whole.1 = (bf16[256,2048]{1,0:T(8,128)(2,1)}, bf16[256,1024]{1,0:T(8,128)(2,1)}, bf16[256,1024]{1,0:T(8,128)(2,1)}, bf16[256,1024]{1,0:T(8,128)(2,1)}, bf16[256...) custom-call(bf16[256,2048]{1,0:T(8,128)(2,1)} %bitcast.14, ...), custom_call_target="tpu_custom_call" | custom-call | tf_op jit(solution)/shard_map/whole/pallas_call | solution.py:556
  105.1 0.0 copy-start.4
  105.1 2.4 %copy.26 = bf16[1,2,128,2048]{3,2,1,0:T(8,128)(2,1)} copy(bf16[1,2,128,2048]{3,2,1,0:T(8,128)(2,1)} %bitcast.13) | data formatting | bytes 2097152
  107.5 0.0 copy-done.4
  107.5 0.0 copy-start.3
  107.5 0.8 copy.27
  108.2 0.4 copy-done.3
  108.7 0.0 copy-start.2
  108.7 0.8 copy.28
  109.5 0.4 copy-done.2
  109.9 0.0 copy-start.1
  109.9 0.8 copy.29
  110.7 0.4 copy-done.1
  111.1 0.0 copy-start
  111.2 0.8 copy.30
  111.9 0.4 copy-done
  112.4 0.0 copy-start.6
  112.4 0.8 copy.31
  113.2 0.2 copy-done.6
  113.4 0.0 copy-start.5
  113.4 0.7 copy.32
  114.1 0.3 copy-done.5
  114.4 0.7 copy.33
Async XLA Ops:
  0.6 0.7 copy-start.7
  105.1 2.4 %copy-start.4 = (bf16[256,1024]{1,0:T(8,128)(2,1)S(1)}, bf16[256,1024]{1,0:T(8,128)(2,1)}, u32[]{:S(2)}) copy-start(bf16[256,1024]{1,0:T(8,128)(2,1)} %get-tuple-element.17) | copy-start | bytes 1572868
  107.5 1.2 %copy-start.3 = (bf16[256,1024]{1,0:T(8,128)(2,1)S(1)}, bf16[256,1024]{1,0:T(8,128)(2,1)}, u32[]{:S(2)}) copy-start(bf16[256,1024]{1,0:T(8,128)(2,1)} %get-tuple-element.18) | copy-start | bytes 1572868
  108.7 1.2 %copy-start.2 = (bf16[256,1024]{1,0:T(8,128)(2,1)S(1)}, bf16[256,1024]{1,0:T(8,128)(2,1)}, u32[]{:S(2)}) copy-start(bf16[256,1024]{1,0:T(8,128)(2,1)} %get-tuple-element.19) | copy-start | bytes 1572868
  109.9 1.2 %copy-start.1 = (bf16[256,1024]{1,0:T(8,128)(2,1)S(1)}, bf16[256,1024]{1,0:T(8,128)(2,1)}, u32[]{:S(2)}) copy-start(bf16[256,1024]{1,0:T(8,128)(2,1)} %get-tuple-element.20) | copy-start | bytes 1572868
  111.1 1.2 %copy-start = (bf16[256,1024]{1,0:T(8,128)(2,1)S(1)}, bf16[256,1024]{1,0:T(8,128)(2,1)}, u32[]{:S(2)}) copy-start(bf16[256,1024]{1,0:T(8,128)(2,1)} %get-tuple-element.21) | copy-start | bytes 1572868
  112.4 1.0 copy-start.6
  113.4 1.0 copy-start.5

commit v2 on v1

--- a/solution.py
+++ b/solution.py
@@ -31,13 +31,28 @@
 
 
 def kernel(
-    patches, q_rows, k_rows, v_rows, w_out, gain, w_val, q_cols, k_cols, cotangent,
+    h_patches, h_q_rows, h_k_rows, h_v_rows, h_w_out, h_gain, h_w_val, h_q_cols, h_k_cols, h_cot,
     g_patches, g_qrow, g_krow, g_vrow, g_qcol, g_kcol, g_wout, g_wval,
     Wo, Wv, p_rows, p_cols, att2, gv_col, gv_in, gv_row, gv2, resid, inverse, normed2, scaled,
     val_out, val_in, gp2, g_att,
     Go, Gv, to, tv, so, sv, uo, uv, zo, zv, fo, fv, oo, ov,
-    send_sems, recv_sems, local_sems,
+    patches, q_rows, k_rows, v_rows, w_out, gain_in, w_val, q_cols, k_cols, cotangent, gain,
+    send_sems, recv_sems, local_sems, load_sems,
 ):
+    loads = {}
+    for i, (name, source, target) in enumerate((
+        ("w_out", h_w_out, w_out), ("w_val", h_w_val, w_val), ("q_cols", h_q_cols, q_cols),
+        ("k_cols", h_k_cols, k_cols), ("cotangent", h_cot, cotangent), ("q_rows", h_q_rows, q_rows),
+        ("k_rows", h_k_rows, k_rows), ("v_rows", h_v_rows, v_rows), ("gain", h_gain, gain_in),
+        ("patches", h_patches, patches),
+    )):
+        loads[name] = pltpu.make_async_copy(source, target, load_sems.at[i])
+        loads[name].start()
+
+    def loaded(*names):
+        for name in names:
+            loads[name].wait()
+
     x, f, r = lax.axis_index("dp"), lax.axis_index("fsdp"), lax.axis_index("row")
     y, zl, c = r // 4, (r // 2) % 2, r % 2
     z = f * 2 + zl
@@ -347,41 +362,47 @@
     def block(ref, k):
         return ref.at[pl.ds(pl.multiple_of(((r + k) % 16) * 16, 16), 16)]
 
-    gather_o.start_z()
-    gather_v.start_z()
-    lax.fori_loop(0, 4, col_forward, 0)
-    gather_o.start_two()
-    gather_v.start_two()
-    lax.fori_loop(4, 8, col_forward, 0)
-    for k in range(1, 16):
-        send(block(gv_col, k), block(gv_in, 0), at_row(k), s_gv + k - 1)
+    def rows_forward(i):
+        if i == 0:
+            loaded("q_rows", "k_rows", "v_rows")
+        lax.fori_loop(4 * i, 4 * i + 4, row_forward, 0, unroll=4)
+
+    def cols_forward(i):
+        if i == 0:
+            loaded("q_cols", "k_cols", "cotangent")
+        lax.fori_loop(2 * i, 2 * i + 2, col_forward, 0, unroll=2)
+
+    def rows_backward(i):
+        lax.fori_loop(4 * i, 4 * i + 4, row_backward, 0, unroll=4)
+
+    def cols_backward(i):
+        lax.fori_loop(2 * i, 2 * i + 2, col_backward, 0, unroll=2)
+
     keep_gv = pltpu.make_async_copy(block(gv_col, 0), block(gv_in, 0), local_sems.at[4])
-    keep_gv.start()
-    gather_o.start_one()
-    lax.fori_loop(0, 8, row_forward, 0)
-    gather_o.forward()
-    gather_v.start_one()
-    lax.fori_loop(8, 16, row_forward, 0)
-    send(att2.at[c], att2.at[c], sibling, s_act)
-    gather_o.nearer()
-
-    keep_gv.wait()
-    for k in range(1, 16):
-        arrived(block(gv_in, 16 - k), s_gv + k - 1)
-    for piece in range(0, HW, 256):
-        cols = slice(piece, piece + 256)
-        moved = gv_in[:, cols].astype(F32).reshape(16, 2, 8, 256)
-        for s in range(2):
-            gv_row[128 * s : 128 * s + 128, cols] = moved[:, s].reshape(128, 256).astype(BF16)
+    keep_val = pltpu.make_async_copy(block(val_out, 0), block(val_in, 0), local_sems.at[5])
+
+    def send_gv():
+        for k in range(1, 16):
+            send(block(gv_col, k), block(gv_in, 0), at_row(k), s_gv + k - 1)
+        keep_gv.start()
 
     def half(k, n):
         return pl.ds(pl.multiple_of(((c + k) % 2) * n, 128), n)
 
-    send(gv_row.at[:, half(1, HW // 2)], gv2.at[c], sibling, s_act + 1)
-    gv2[c] = gv_row[:, half(0, HW // 2)]
-
-    gather_o.farther()
-    gather_o.finish()
+    def take_gv():
+        keep_gv.wait()
+        for k in range(1, 16):
+            arrived(block(gv_in, 16 - k), s_gv + k - 1)
+        for piece in range(0, HW, 256):
+            cols = slice(piece, piece + 256)
+            moved = gv_in[:, cols].astype(F32).reshape(16, 2, 8, 256)
+            for s in range(2):
+                gv_row[128 * s : 128 * s + 128, cols] = moved[:, s].reshape(128, 256).astype(BF16)
+        send(gv_row.at[:, half(1, HW // 2)], gv2.at[c], sibling, s_act + 1)
+        gv2[c] = gv_row[:, half(0, HW // 2)]
+
+    def send_att():
+        send(att2.at[c], att2.at[c], sibling, s_act)
 
     def residual_tile(i, _):
         cols = pl.ds(pl.multiple_of(i * 512, 512), 512)
@@ -389,47 +410,48 @@
         resid[:, cols] = (dot(att2[c], weight, 1, 0) + patches[:, cols].astype(F32)).astype(BF16)
         return 0
 
-    lax.fori_loop(0, D // 512, residual_tile, 0)
-    gather_v.forward()
+    def residual():
+        loaded("patches")
+        lax.fori_loop(0, D // 512, residual_tile, 0)
 
     def norm_rows(i, _):
         rows = pl.ds(pl.multiple_of(i * 16, 16), 16)
         stream = resid[rows, :].astype(F32)
         inv = lax.rsqrt(jnp.mean(stream * stream, axis=-1, keepdims=True) + 1e-05)
         inverse[rows, :] = jnp.broadcast_to(inv, (16, 128))
-        normed2[c, rows, :] = (stream * inv * gain[...].astype(F32)).astype(BF16)
-        return 0
-
-    lax.fori_loop(0, T // 16, norm_rows, 0)
-    send(normed2.at[c], normed2.at[c], sibling, s_act + 2)
-    gather_v.nearer()
-    arrived(gv2.at[1 - c], s_act + 1)
-    arrived(normed2.at[1 - c], s_act + 2)
+        normed2[c, rows, :] = (stream * inv * gain[...]).astype(BF16)
+        return 0
+
+    def norm():
+        loaded("gain")
+        gain_rows = gain_in[...].astype(F32)
+        for i in range(D // 128):
+            gain[:, 128 * i : 128 * i + 128] = gain_rows[i : i + 1, :]
+        lax.fori_loop(0, T // 16, norm_rows, 0, unroll=4)
+        send(normed2.at[c], normed2.at[c], sibling, s_act + 2)
 
     def wval_tile(i, _):
         left = normed2[:, :, pl.ds(pl.multiple_of(i * 512, 512), 512)].reshape(2 * T, 512)
         Gv[i] = dot(left, gv2[...].reshape(2 * T, 512), 0, 0).astype(BF16).reshape(4, 2, 2, 32, 512)
         return 0
 
-    lax.fori_loop(0, 2, wval_tile, 0)
-    scatter_v.start_one(0)
-    lax.fori_loop(2, 4, wval_tile, 0)
-    scatter_v.start_one(1)
-    gather_v.farther()
-    gather_v.finish()
-
-    scaled_sum = jnp.zeros((T, 128), F32)
+    def wval(part):
+        if part == 0:
+            arrived(gv2.at[1 - c], s_act + 1)
+            arrived(normed2.at[1 - c], s_act + 2)
+        lax.fori_loop(2 * part, 2 * part + 2, wval_tile, 0)
+        scatter_v.start_one(part)
 
     def normed_grad_tile(i, total):
         cols = pl.ds(pl.multiple_of(i * 512, 512), 512)
         weight = Wv[i].reshape(512, HW)
-        grad = dot(gv_row[...], weight, 1, 1) * gain[:, cols].astype(F32)
+        grad = dot(gv_row[...], weight, 1, 1) * gain[:, cols]
         scaled[:, cols] = grad
         product = grad * resid[:, cols].astype(F32)
         return total + sum(product[:, 128 * k : 128 * k + 128] for k in range(4))
 
-    scaled_sum = lax.fori_loop(0, 4, normed_grad_tile, scaled_sum)
-    scaled[:, D:] = scaled_sum
+    def normed_grad():
+        scaled[:, D:] = lax.fori_loop(0, 4, normed_grad_tile, jnp.zeros((T, 128), F32))
 
     def stream_rows(i, _):
         rows = pl.ds(pl.multiple_of(i * 16, 16), 16)
@@ -440,23 +462,22 @@
         g_patches[rows, :] = result.astype(BF16)
         return 0
 
-    lax.fori_loop(0, T // 16, stream_rows, 0)
-    send(g_patches.at[:, half(1, D // 2)], gp2.at[c], sibling, s_act + 3)
-    gp2[c] = g_patches[:, half(0, D // 2)]
-    scatter_v.merge(0)
-    scatter_v.merge(1)
-    arrived(att2.at[1 - c], s_act)
-    arrived(gp2.at[1 - c], s_act + 3)
+    def stream_grad():
+        lax.fori_loop(0, T // 16, stream_rows, 0, unroll=4)
+        send(g_patches.at[:, half(1, D // 2)], gp2.at[c], sibling, s_act + 3)
+        gp2[c] = g_patches[:, half(0, D // 2)]
 
     def wout_tile(i, _):
         left = att2[:, :, pl.ds(pl.multiple_of(i * 256, 256), 256)].reshape(2 * T, 256)
         Go[i] = dot(left, gp2[...].reshape(2 * T, HW), 0, 0).astype(BF16).reshape(4, 2, 2, 16, HW)
         return 0
 
-    lax.fori_loop(0, 2, wout_tile, 0)
-    scatter_o.start_one(0)
-    lax.fori_loop(2, 4, wout_tile, 0)
-    scatter_o.start_one(1)
+    def wout(part):
+        if part == 0:
+            arrived(att2.at[1 - c], s_act)
+            arrived(gp2.at[1 - c], s_act + 3)
+        lax.fori_loop(2 * part, 2 * part + 2, wout_tile, 0)
+        scatter_o.start_one(part)
 
     def values_tile(i, _):
         cols = pl.ds(pl.multiple_of(i * 256, 256), 256)
@@ -466,14 +487,16 @@
         val_out[:, cols] = both.reshape(T, 256).astype(BF16)
         return 0
 
-    lax.fori_loop(0, HW // 256, values_tile, 0)
-    for k in range(1, 16):
-        send(block(val_out, k), block(val_in, 0), at_row(k), s_val + k - 1)
-    keep_val = pltpu.make_async_copy(block(val_out, 0), block(val_in, 0), local_sems.at[5])
-    keep_val.start()
-
-    scatter_v.start_two(0)
-    scatter_v.start_two(1)
+    def send_values():
+        lax.fori_loop(0, HW // 256, values_tile, 0)
+        for k in range(1, 16):
+            send(block(val_out, k), block(val_in, 0), at_row(k), s_val + k - 1)
+        keep_val.start()
+
+    def take_values():
+        keep_val.wait()
+        for k in range(1, 16):
+            arrived(block(val_in, 16 - k), s_val + k - 1)
 
     def att_grad_tile(i, _):
         weight = Wo[i].reshape(256, D)
@@ -482,30 +505,83 @@
         ).astype(BF16)
         return 0
 
-    lax.fori_loop(0, 4, att_grad_tile, 0)
+    def att_grad():
+        lax.fori_loop(0, 4, att_grad_tile, 0)
+
+    loaded("w_val")
+    gather_v.start_z()
+    rows_forward(0)
+    rows_forward(1)
+    loaded("w_out")
+    gather_o.start_z()
+    cols_forward(0)
+    gather_v.start_two()
+    gather_o.start_two()
+    rows_forward(2)
+    gather_v.start_one()
+    cols_forward(1)
+    gather_o.start_one()
+    rows_forward(3)
+    gather_o.forward()
+    cols_forward(2)
+    gather_o.nearer()
+    gather_v.forward()
+    cols_forward(3)
+    gather_o.farther()
+    send_gv()
+    gather_v.nearer()
+    send_att()
+    gather_v.farther()
+    gather_o.finish()
+    residual()
+    norm()
+    gather_v.finish()
+    send_values()
+    take_gv()
+    normed_grad()
+    wval(0)
+    wval(1)
+    stream_grad()
+    wout(0)
+    wout(1)
+    att_grad()
+    scatter_v.merge(1)
+    scatter_v.merge(0)
     scatter_o.merge(0)
     scatter_o.merge(1)
-    lax.fori_loop(0, 8, row_backward, 0)
+    rows_backward(0)
+    take_values()
+    scatter_v.start_two(1)
+    scatter_v.start_two(0)
+    rows_backward(1)
+    scatter_o.start_two(1)
+    scatter_o.start_two(0)
+    scatter_v.end_two(1)
     scatter_v.end_two(0)
-    scatter_v.end_two(1)
     scatter_v.start_three()
-    lax.fori_loop(8, 16, row_backward, 0)
-    scatter_o.start_two(0)
-    scatter_o.start_two(1)
+    cols_backward(0)
+    scatter_o.end_two(1)
+    scatter_o.end_two(0)
+    scatter_o.start_three()
+    cols_backward(1)
+    rows_backward(2)
     scatter_v.start_four()
-    keep_val.wait()
-    for k in range(1, 16):
-        arrived(block(val_in, 16 - k), s_val + k - 1)
-    lax.fori_loop(0, 4, col_backward, 0)
-    scatter_o.end_two(0)
-    scatter_o.end_two(1)
-    scatter_o.start_three()
-    lax.fori_loop(4, 8, col_backward, 0)
+    cols_backward(2)
+    scatter_o.start_four()
+    rows_backward(3)
+    cols_backward(3)
+    scatter_o.finish()
     scatter_v.finish()
-    scatter_o.start_four()
-    scatter_o.finish()
     for copy in sent:
         copy.wait_send()
+
+
+def place_results(*refs):
+    copies = [pltpu.make_async_copy(refs[i], refs[8 + i], refs[16].at[i]) for i in range(8)]
+    for copy in copies:
+        copy.start()
+    for copy in copies:
+        copy.wait()
 
 
 def body(patches, q_rows, k_rows, v_rows, w_out, gain, w_val, q_cols, k_cols, cotangent):
@@ -548,26 +624,41 @@
     ]
     for a, b in zip(ro, rv):
         scratch += [a, b]
+    inputs = [(T, D), (T, HW), (T, HW), (T, HW), (16, D), (D // 128, 128), (32, HW)] + [(T, HW)] * 3
+    scratch += [pltpu.VMEM(shape, BF16) for shape in inputs] + [pltpu.VMEM((1, D), F32)]
     scratch += [
         pltpu.SemaphoreType.DMA((COPIES,)),
         pltpu.SemaphoreType.DMA((COPIES,)),
         pltpu.SemaphoreType.DMA((6,)),
+        pltpu.SemaphoreType.DMA((10,)),
     ]
+    operands = (
+        patches.reshape(T, D), q_rows.reshape(T, HW), k_rows.reshape(T, HW),
+        v_rows.reshape(T, HW), w_out, gain.reshape(D // 128, 128), w_val, q_cols.reshape(T, HW),
+        k_cols.reshape(T, HW), cotangent.reshape(T, HW),
+    )
+    operands = [pltpu.with_memory_space_constraint(a, pltpu.HBM) for a in operands]
     results = pl.pallas_call(
         kernel,
         out_shape=out_shape,
-        in_specs=[vmem] * 10,
+        in_specs=[pl.BlockSpec(memory_space=pltpu.HBM)] * 10,
         out_specs=[vmem] * 8,
         scratch_shapes=scratch,
         compiler_params=pltpu.CompilerParams(
-            collective_id=0, has_side_effects=True, vmem_limit_bytes=56 * 2**20
+            collective_id=0, has_side_effects=True, vmem_limit_bytes=46 * 2**20
         ),
         name="whole",
-    )(
-        patches.reshape(T, D), q_rows.reshape(T, HW), k_rows.reshape(T, HW),
-        v_rows.reshape(T, HW), w_out, gain.reshape(1, D), w_val, q_cols.reshape(T, HW),
-        k_cols.reshape(T, HW), cotangent.reshape(T, HW),
-    )
+    )(*operands)
+    anywhere = pl.BlockSpec(memory_space=pl.ANY)
+    results = pl.pallas_call(
+        place_results,
+        out_shape=out_shape,
+        in_specs=[anywhere] * 8,
+        out_specs=[pl.BlockSpec(memory_space=pltpu.HBM)] * 8,
+        scratch_shapes=[pltpu.SemaphoreType.DMA((8,))],
+        compiler_params=pltpu.CompilerParams(vmem_limit_bytes=2**20),
+        name="place",
+    )(*results)
     return (
         results[0].reshape(patches.shape),
         *(results[i].reshape(q_rows.shape) for i in range(1, 4)),

time: 115 us -> 97.4 us (0.85)
  local copies, waits for them, and re-layouts: 11.2 us -> 0 us
  Pallas kernels: 103 us -> 96.5 us
    unnamed x24 -> x0, local copies, waits for them, and re-layouts: 10.6 us -> none
    pallas_call x1 -> x2, Pallas kernels: 103 us -> 96.5 us  [the longest x1 94.5 us: body(): pl.pallas_call(kernel, out_shape=out_shape, in_specs=[pl.BlockSpec(memory...]
where the time goes in v2:
time: 97.4 us; the launch traced here: 97.3 us
  Pallas kernels  96.5 us (99%)
    pallas_call x1, Pallas kernels, body(): pl.pallas_call(kernel, out_shape=out_shape, in_specs=[pl.BlockSpec(memory...  94.5 us
    pallas_call x1, Pallas kernels, body(): pl.pallas_call(place_results, out_shape=out_shape, in_specs=[anywhere] *...  1.98 us

profile of v2, /device:TPU:1, one launch (start us, length us, event | category | flops | bytes accessed | tf_op | source)
XLA Modules:
  0.0 97.3 jit_solution(17804014966853051140)
XLA Ops:
  0.6 94.5 %whole.1 = (bf16[256,2048]{1,0:T(8,128)(2,1)S(1)}, bf16[256,1024]{1,0:T(8,128)(2,1)S(1)}, bf16[256,1024]{1,0:T(8,128)(2,1)S(1)}, bf16[256,1024]{1,0:T(8,128)(2,1...) custom-call(bf16[256,2048]{1,0:T(8,128)(2,1)} %bitcast.14, ...), custom_call_target="tpu_custom_call" | custom-call | tf_op jit(solution)/shard_map/whole/pallas_call | solution.py:641
  95.2 2.0 %place.1 = (bf16[256,2048]{1,0:T(8,128)(2,1)}, bf16[256,1024]{1,0:T(8,128)(2,1)}, bf16[256,1024]{1,0:T(8,128)(2,1)}, bf16[256,1024]{1,0:T(8,128)(2,1)}, bf16[256...) custom-call(bf16[256,2048]{1,0:T(8,128)(2,1)S(1)} %get-tuple-element.24.refs_0_, ...), custom_call_target="tpu_custom_call" | custom-call | tf_op jit(solution)/shard_map/place/pallas_call | solution.py:653

commit v3 on v2

--- a/solution.py
+++ b/solution.py
@@ -13,7 +13,8 @@
 D = 2048
 HW = 1024
 T = 256
-COPIES = 256
+SENDS = 26
+RECVS = 72
 SCALE = 1.0 / math.sqrt(HD)
 MESH = pl.DeviceIdType.MESH
 F32 = jnp.float32
@@ -36,7 +37,7 @@
     Wo, Wv, p_rows, p_cols, att2, gv_col, gv_in, gv_row, gv2, resid, inverse, normed2, scaled,
     val_out, val_in, gp2, g_att,
     Go, Gv, to, tv, so, sv, uo, uv, zo, zv, fo, fv, oo, ov,
-    patches, q_rows, k_rows, v_rows, w_out, gain_in, w_val, q_cols, k_cols, cotangent, gain,
+    patches, q_rows, k_rows, v_rows, w_out, gain_in, w_val, q_cols, k_cols, cotangent, gain, spare,
     send_sems, recv_sems, local_sems, load_sems,
 ):
     loads = {}
@@ -82,34 +83,46 @@
         pl.semaphore_signal(barrier, inc=1, device_id=peer, device_id_type=MESH)
     pl.semaphore_wait(barrier, len(peers))
 
-    used = [0]
-    sent = []
-
-    def slots(n):
-        first = used[0]
-        used[0] += n
-        assert used[0] <= COPIES
+    counts = {"send": 0, "recv": 0}
+    sent = {}
+
+    def slots(kind, n):
+        first = counts[kind]
+        counts[kind] += n
+        assert counts[kind] <= (SENDS if kind == "send" else RECVS)
         return first
 
-    def remote(src, dst, where, i):
+    def remote(src, dst, where, i, g):
         return pltpu.make_async_remote_copy(
-            src_ref=src, dst_ref=dst, send_sem=send_sems.at[i], recv_sem=recv_sems.at[i],
+            src_ref=src, dst_ref=dst, send_sem=send_sems.at[g], recv_sem=recv_sems.at[i],
             device_id=where, device_id_type=MESH,
         )
 
-    def send(src, dst, where, i):
-        copy = remote(src, dst, where, i)
-        copy.start()
-        sent.append(copy)
+    def size(ref):
+        return math.prod(ref.shape) * jnp.dtype(ref.dtype).itemsize
+
+    def send(src, dst, where, i, g):
+        remote(src, dst, where, i, g).start()
+        sent[g] = sent.get(g, 0) + size(src)
+
+    def span(total):
+        assert total % 4096 == 0 and total <= 2**20
+        return spare.at[0 : total // 256]
 
     def arrived(region, i):
-        remote(region, region, sibling, i).wait_recv()
+        remote(region, region, sibling, i, 0).wait_recv()
+
+    def all_arrived(total, i):
+        remote(span(total), span(total), sibling, i, 0).wait_recv()
 
     class Gather:
         def __init__(self, W, own, cols, local):
             self.W, self.own, self.q = W, own, cols // 4
             self.local = local
-            self.z, self.two, self.one, self.sib = slots(7), slots(6), slots(12), slots(16)
+            self.z, self.two = slots("recv", 1), slots("recv", 2)
+            self.one, self.sib = slots("recv", 12), slots("recv", 2)
+            self.sz, self.s1, self.ss = slots("send", 1), slots("send", 2), slots("send", 2)
+            self.block = size(own)
 
         def quarter(self, k):
             return pl.ds(pl.multiple_of(((x + k) % 4) * self.q, 128), self.q)
@@ -120,51 +133,39 @@
             self.keep = pltpu.make_async_copy(mine, there, local_sems.at[self.local])
             self.keep.start()
             for k in range(1, 8):
-                send(mine, there, at_z(k), self.z + k - 1)
+                send(mine, there, at_z(k), self.z, self.sz)
 
         def start_two(self):
             self.keep.wait()
-            for k in range(1, 8):
-                pz = (z + 8 - k) % 8
-                arrived(self.W.at[pz // 2, y, pz % 2, c, :, self.quarter(0)], self.z + k - 1)
+            all_arrived(7 * self.block // 4, self.z)
             for part in range(2):
                 block = self.W.at[pl.ds(2 * part, 2), y, :, c, :, self.quarter(0)]
                 for k in range(1, 4):
-                    send(block, block, (at_x if part == 0 else at_y)(k), self.two + 3 * part + k - 1)
+                    send(block, block, (at_x if part == 0 else at_y)(k), self.two + part, self.sz)
 
         def chunk(self, part, j, k):
             if part == 0:
                 return self.W.at[j, (y + k) % 4, :, c, :, :]
             return self.W.at[2 + j, :, :, c, :, self.quarter(k)]
 
-        def other(self, part, j, k):
-            if part == 0:
-                return self.W.at[j, (y + k) % 4, :, 1 - c, :, :]
-            return self.W.at[2 + j, :, :, 1 - c, :, self.quarter(k)]
-
-        def share(self, part, j, k, i):
+        def share(self, part, j, k):
             block = self.chunk(part, j, k)
-            send(block, block, sibling, self.sib + 8 * part + i)
+            send(block, block, sibling, self.sib + part, self.ss + part)
 
         def start_one(self):
             for part in range(2):
-                for k in range(1, 4):
-                    if part == 0:
-                        region = self.W.at[pl.ds(0, 2), y, :, c, :, self.quarter(4 - k)]
-                    else:
-                        region = self.W.at[pl.ds(2, 2), (y + 4 - k) % 4, :, c, :, self.quarter(0)]
-                    arrived(region, self.two + 3 * part + k - 1)
+                all_arrived(3 * self.block, self.two + part)
             for part in range(2):
                 at = at_y if part == 0 else at_x
                 first = self.one + 6 * part
                 a, b = self.chunk(part, 0, 0), self.chunk(part, 1, 0)
-                send(a, a, at(1), first)
-                send(b, b, at(3), first + 1)
-                send(b, b, at(1), first + 2)
-                send(a, a, at(3), first + 3)
-            for part in range(2):
-                self.share(part, 0, 0, 0)
-                self.share(part, 1, 0, 1)
+                send(a, a, at(1), first, self.s1 + part)
+                send(b, b, at(3), first + 1, self.s1 + part)
+                send(b, b, at(1), first + 2, self.s1 + part)
+                send(a, a, at(3), first + 3, self.s1 + part)
+            for part in range(2):
+                self.share(part, 0, 0)
+                self.share(part, 1, 0)
 
         def forward(self):
             for part in range(2):
@@ -172,39 +173,41 @@
                 first = self.one + 6 * part
                 a, b = self.chunk(part, 0, 3), self.chunk(part, 1, 1)
                 arrived(a, first)
-                send(a, a, at(1), first + 4)
-                self.share(part, 0, 3, 2)
+                send(a, a, at(1), first + 4, self.s1 + part)
+                self.share(part, 0, 3)
                 arrived(b, first + 1)
-                send(b, b, at(3), first + 5)
-                self.share(part, 1, 1, 3)
+                send(b, b, at(3), first + 5, self.s1 + part)
+                self.share(part, 1, 1)
 
         def nearer(self):
             for part in range(2):
                 first = self.one + 6 * part
                 arrived(self.chunk(part, 1, 3), first + 2)
-                self.share(part, 1, 3, 4)
+                self.share(part, 1, 3)
                 arrived(self.chunk(part, 0, 1), first + 3)
-                self.share(part, 0, 1, 5)
+                self.share(part, 0, 1)
 
         def farther(self):
             for part in range(2):
                 first = self.one + 6 * part
                 arrived(self.chunk(part, 0, 2), first + 4)
-                self.share(part, 0, 2, 6)
+                self.share(part, 0, 2)
                 arrived(self.chunk(part, 1, 2), first + 5)
-                self.share(part, 1, 2, 7)
+                self.share(part, 1, 2)
 
         def finish(self):
-            order = ((0, 0), (1, 0), (0, 3), (1, 1), (1, 3), (0, 1), (0, 2), (1, 2))
-            for part in range(2):
-                for i, (j, k) in enumerate(order):
-                    arrived(self.other(part, j, k), self.sib + 8 * part + i)
+            for part in range(2):
+                all_arrived(16 * self.block, self.sib + part)
 
     class Scatter:
         def __init__(self, G, t, s, u, zb, fin, o, out, rows, cols, local):
             self.G, self.t, self.s, self.u, self.zb, self.fin, self.o = G, t, s, u, zb, fin, o
             self.out, self.rows, self.q, self.local = out, rows, cols // 8, local
-            self.one, self.two, self.three, self.four = slots(12), slots(6), slots(7), slots(7)
+            self.one, self.two = slots("recv", 12), slots("recv", 2)
+            self.three, self.four = slots("recv", 1), slots("recv", 1)
+            self.s1, self.s2 = slots("send", 2), slots("send", 1)
+            self.s3, self.s4 = slots("send", 1), slots("send", 1)
+            self.block = 2 * rows * cols
 
         def quarter(self, k):
             return pl.ds(pl.multiple_of(((x + k) % 4) * self.q, 128), self.q)
@@ -218,10 +221,10 @@
             at = at_y if part == 0 else at_x
             first = self.one + 6 * part
             t, s = self.t[part], self.s[part]
-            send(self.chunk(part, 0, 2), t.at[0], at(1), first)
-            send(self.chunk(part, 1, 2), t.at[1], at(3), first + 1)
-            send(self.chunk(part, 1, 1), s.at[0, 1], at(1), first + 2)
-            send(self.chunk(part, 0, 3), s.at[1, 0], at(3), first + 3)
+            send(self.chunk(part, 0, 2), t.at[0], at(1), first, self.s1 + part)
+            send(self.chunk(part, 1, 2), t.at[1], at(3), first + 1, self.s1 + part)
+            send(self.chunk(part, 1, 1), s.at[0, 1], at(1), first + 2, self.s1 + part)
+            send(self.chunk(part, 0, 3), s.at[1, 0], at(3), first + 3, self.s1 + part)
 
         def add_into(self, target, others):
             for lead in range(target.shape[0]):
@@ -236,10 +239,10 @@
             t, s = self.t[part], self.s[part]
             arrived(t.at[0], first)
             self.add_into(self.chunk(part, 0, 1), [t.at[0]])
-            send(self.chunk(part, 0, 1), s.at[0, 0], at(1), first + 4)
+            send(self.chunk(part, 0, 1), s.at[0, 0], at(1), first + 4, self.s1 + part)
             arrived(t.at[1], first + 1)
             self.add_into(self.chunk(part, 1, 3), [t.at[1]])
-            send(self.chunk(part, 1, 3), s.at[1, 1], at(3), first + 5)
+            send(self.chunk(part, 1, 3), s.at[1, 1], at(3), first + 5, self.s1 + part)
 
         def piece(self, part, k):
             if part == 0:
@@ -258,12 +261,11 @@
             for k in range(1, 4):
                 send(
                     self.piece(part, k), self.u.at[part, k - 1],
-                    (at_x if part == 0 else at_y)(k), self.two + 3 * part + k - 1,
+                    (at_x if part == 0 else at_y)(k), self.two + part, self.s2,
                 )
 
         def end_two(self, part):
-            for k in range(1, 4):
-                arrived(self.u.at[part, k - 1], self.two + 3 * part + k - 1)
+            all_arrived(3 * self.block, self.two + part)
             self.add_into(self.piece(part, 0), [self.u.at[part, k] for k in range(3)])
 
         def start_three(self):
@@ -271,12 +273,11 @@
                 pz = (z + k) % 8
                 send(
                     self.G.at[pz // 2, y, pz % 2, :, :, self.quarter(0)], self.zb.at[k - 1],
-                    at_z(k), self.three + k - 1,
+                    at_z(k), self.three, self.s3,
                 )
 
         def start_four(self):
-            for k in range(1, 8):
-                arrived(self.zb.at[k - 1], self.three + k - 1)
+            all_arrived(7 * self.block // 4, self.three)
             for pc in range(2):
                 total = self.G[f, y, zl, pc, :, self.quarter(0)].astype(F32)
                 for k in range(7):
@@ -292,17 +293,12 @@
                         pc = (c + s) % 2
                         send(
                             self.fin.at[pc], self.o.at[c, x], place((x + k) % 4, y, z, pc),
-                            self.four + 2 * k + s - 1,
+                            self.four, self.s4,
                         )
 
         def finish(self):
             self.keep.wait()
-            for k in range(4):
-                for s in range(2):
-                    if k or s:
-                        arrived(
-                            self.o.at[(c + s) % 2, (x + 4 - k) % 4], self.four + 2 * k + s - 1
-                        )
+            all_arrived(7 * self.block // 4, self.four)
             for pc in range(2):
                 for px in range(4):
                     first = (4 * pc + px) * self.q
@@ -312,7 +308,8 @@
     gather_v = Gather(Wv, w_val, HW, 1)
     scatter_o = Scatter(Go, to, so, uo, zo, fo, oo, g_wout, 16, D, 2)
     scatter_v = Scatter(Gv, tv, sv, uv, zv, fv, ov, g_wval, 32, HW, 3)
-    s_gv, s_val, s_act = slots(15), slots(15), slots(4)
+    s_gv, s_val, s_act = slots("recv", 1), slots("recv", 1), slots("recv", 4)
+    t_gv, t_val, t_act = slots("send", 1), slots("send", 1), slots("send", 4)
 
     def head(h):
         return pl.ds(pl.multiple_of(h * HD, HD), HD)
@@ -383,7 +380,7 @@
 
     def send_gv():
         for k in range(1, 16):
-            send(block(gv_col, k), block(gv_in, 0), at_row(k), s_gv + k - 1)
+            send(block(gv_col, k), block(gv_in, 0), at_row(k), s_gv, t_gv)
         keep_gv.start()
 
     def half(k, n):
@@ -391,18 +388,17 @@
 
     def take_gv():
         keep_gv.wait()
-        for k in range(1, 16):
-            arrived(block(gv_in, 16 - k), s_gv + k - 1)
+        all_arrived(15 * 32 * HW, s_gv)
         for piece in range(0, HW, 256):
             cols = slice(piece, piece + 256)
             moved = gv_in[:, cols].astype(F32).reshape(16, 2, 8, 256)
             for s in range(2):
                 gv_row[128 * s : 128 * s + 128, cols] = moved[:, s].reshape(128, 256).astype(BF16)
-        send(gv_row.at[:, half(1, HW // 2)], gv2.at[c], sibling, s_act + 1)
+        send(gv_row.at[:, half(1, HW // 2)], gv2.at[c], sibling, s_act + 1, t_act + 1)
         gv2[c] = gv_row[:, half(0, HW // 2)]
 
     def send_att():
-        send(att2.at[c], att2.at[c], sibling, s_act)
+        send(att2.at[c], att2.at[c], sibling, s_act, t_act)
 
     def residual_tile(i, _):
         cols = pl.ds(pl.multiple_of(i * 512, 512), 512)
@@ -428,7 +424,7 @@
         for i in range(D // 128):
             gain[:, 128 * i : 128 * i + 128] = gain_rows[i : i + 1, :]
         lax.fori_loop(0, T // 16, norm_rows, 0, unroll=4)
-        send(normed2.at[c], normed2.at[c], sibling, s_act + 2)
+        send(normed2.at[c], normed2.at[c], sibling, s_act + 2, t_act + 2)
 
     def wval_tile(i, _):
         left = normed2[:, :, pl.ds(pl.multiple_of(i * 512, 512), 512)].reshape(2 * T, 512)
@@ -464,7 +460,7 @@
 
     def stream_grad():
         lax.fori_loop(0, T // 16, stream_rows, 0, unroll=4)
-        send(g_patches.at[:, half(1, D // 2)], gp2.at[c], sibling, s_act + 3)
+        send(g_patches.at[:, half(1, D // 2)], gp2.at[c], sibling, s_act + 3, t_act + 3)
         gp2[c] = g_patches[:, half(0, D // 2)]
 
     def wout_tile(i, _):
@@ -490,13 +486,12 @@
     def send_values():
         lax.fori_loop(0, HW // 256, values_tile, 0)
         for k in range(1, 16):
-            send(block(val_out, k), block(val_in, 0), at_row(k), s_val + k - 1)
+            send(block(val_out, k), block(val_in, 0), at_row(k), s_val, t_val)
         keep_val.start()
 
     def take_values():
         keep_val.wait()
-        for k in range(1, 16):
-            arrived(block(val_in, 16 - k), s_val + k - 1)
+        all_arrived(15 * 32 * HW, s_val)
 
     def att_grad_tile(i, _):
         weight = Wo[i].reshape(256, D)
@@ -572,8 +567,8 @@
     cols_backward(3)
     scatter_o.finish()
     scatter_v.finish()
-    for copy in sent:
-        copy.wait_send()
+    for g, total in sent.items():
+        remote(span(total), span(total), sibling, 0, g).wait_send()
 
 
 def place_results(*refs):
@@ -625,10 +620,10 @@
     for a, b in zip(ro, rv):
         scratch += [a, b]
     inputs = [(T, D), (T, HW), (T, HW), (T, HW), (16, D), (D // 128, 128), (32, HW)] + [(T, HW)] * 3
-    scratch += [pltpu.VMEM(shape, BF16) for shape in inputs] + [pltpu.VMEM((1, D), F32)]
+    scratch += [pltpu.VMEM(shape, BF16) for shape in inputs] + [pltpu.VMEM((1, D), F32), pltpu.VMEM((4096, 128), BF16)]
     scratch += [
-        pltpu.SemaphoreType.DMA((COPIES,)),
-        pltpu.SemaphoreType.DMA((COPIES,)),
+        pltpu.SemaphoreType.DMA((SENDS,)),
+        pltpu.SemaphoreType.DMA((RECVS,)),
         pltpu.SemaphoreType.DMA((6,)),
         pltpu.SemaphoreType.DMA((10,)),
     ]

time: 97.4 us -> 93.3 us (0.958)
  Pallas kernels: 96.5 us -> 92.6 us
    pallas_call x1, Pallas kernels: 94.5 us -> 90.6 us  [body(): pl.pallas_call(kernel, out_shape=out_shape, in_specs=[pl.BlockSpec(memory...]
where the time goes in v3:
time: 93.3 us; the launch traced here: 93.2 us
  Pallas kernels  92.6 us (99%)
    pallas_call x1, Pallas kernels, body(): pl.pallas_call(kernel, out_shape=out_shape, in_specs=[pl.BlockSpec(memory...  90.6 us
    pallas_call x1, Pallas kernels, body(): pl.pallas_call(place_results, out_shape=out_shape, in_specs=[anywhere] *...  1.98 us

profile of v3, /device:TPU:1, one launch (start us, length us, event | category | flops | bytes accessed | tf_op | source)
XLA Modules:
  0.0 93.2 jit_solution(17661697352579961292)
XLA Ops:
  0.6 90.6 %whole.1 = (bf16[256,2048]{1,0:T(8,128)(2,1)S(1)}, bf16[256,1024]{1,0:T(8,128)(2,1)S(1)}, bf16[256,1024]{1,0:T(8,128)(2,1)S(1)}, bf16[256,1024]{1,0:T(8,128)(2,1...) custom-call(bf16[256,2048]{1,0:T(8,128)(2,1)} %bitcast.14, ...), custom_call_target="tpu_custom_call" | custom-call | tf_op jit(solution)/shard_map/whole/pallas_call | solution.py:636
  91.3 2.0 %place.1 = (bf16[256,2048]{1,0:T(8,128)(2,1)}, bf16[256,1024]{1,0:T(8,128)(2,1)}, bf16[256,1024]{1,0:T(8,128)(2,1)}, bf16[256,1024]{1,0:T(8,128)(2,1)}, bf16[256...) custom-call(bf16[256,2048]{1,0:T(8,128)(2,1)S(1)} %get-tuple-element.24.refs_0_, ...), custom_call_target="tpu_custom_call" | custom-call | tf_op jit(solution)/shard_map/place/pallas_call | solution.py:648

commit v4 on v3

--- a/solution.py
+++ b/solution.py
@@ -503,70 +503,70 @@
     def att_grad():
         lax.fori_loop(0, 4, att_grad_tile, 0)
 
-    loaded("w_val")
-    gather_v.start_z()
-    rows_forward(0)
-    rows_forward(1)
     loaded("w_out")
     gather_o.start_z()
     cols_forward(0)
+    cols_forward(1)
+    cols_forward(2)
+    cols_forward(3)
+    send_gv()
+    rows_forward(0)
+    gather_o.start_two()
+    take_gv()
+    loaded("w_val")
+    gather_v.start_z()
+    gather_o.start_one()
+    rows_forward(1)
     gather_v.start_two()
-    gather_o.start_two()
     rows_forward(2)
+    gather_o.forward()
+    gather_o.nearer()
+    rows_forward(3)
     gather_v.start_one()
-    cols_forward(1)
-    gather_o.start_one()
-    rows_forward(3)
-    gather_o.forward()
-    cols_forward(2)
-    gather_o.nearer()
-    gather_v.forward()
-    cols_forward(3)
     gather_o.farther()
-    send_gv()
-    gather_v.nearer()
-    send_att()
-    gather_v.farther()
     gather_o.finish()
     residual()
+    gather_v.forward()
+    gather_v.nearer()
     norm()
+    wval(0)
+    gather_v.farther()
+    wval(1)
     gather_v.finish()
-    send_values()
-    take_gv()
+    send_att()
     normed_grad()
-    wval(0)
-    wval(1)
     stream_grad()
+    scatter_v.merge(0)
+    scatter_v.merge(1)
     wout(0)
     wout(1)
     att_grad()
-    scatter_v.merge(1)
-    scatter_v.merge(0)
-    scatter_o.merge(0)
-    scatter_o.merge(1)
     rows_backward(0)
-    take_values()
+    rows_backward(1)
     scatter_v.start_two(1)
     scatter_v.start_two(0)
-    rows_backward(1)
-    scatter_o.start_two(1)
+    scatter_o.merge(0)
+    rows_backward(2)
+    scatter_o.merge(1)
+    send_values()
     scatter_o.start_two(0)
     scatter_v.end_two(1)
+    rows_backward(3)
+    scatter_o.start_two(1)
     scatter_v.end_two(0)
     scatter_v.start_three()
+    scatter_o.end_two(0)
+    take_values()
     cols_backward(0)
     scatter_o.end_two(1)
-    scatter_o.end_two(0)
     scatter_o.start_three()
     cols_backward(1)
-    rows_backward(2)
     scatter_v.start_four()
     cols_backward(2)
+    cols_backward(3)
+    scatter_v.finish()
     scatter_o.start_four()
-    rows_backward(3)
-    cols_backward(3)
     scatter_o.finish()
-    scatter_v.finish()
     for g, total in sent.items():
         remote(span(total), span(total), sibling, 0, g).wait_send()
 

time: 93.3 us -> 92.3 us (0.989)
  Pallas kernels: 92.6 us -> 91.6 us
    pallas_call x1, Pallas kernels: 90.6 us -> 89.6 us  [body(): pl.pallas_call(kernel, out_shape=out_shape, in_specs=[pl.BlockSpec(memory...]
where the time goes in v4:
time: 92.3 us; the launch traced here: 92.2 us
  Pallas kernels  91.6 us (99%)
    pallas_call x1, Pallas kernels, body(): pl.pallas_call(kernel, out_shape=out_shape, in_specs=[pl.BlockSpec(memory...  89.6 us
    pallas_call x1, Pallas kernels, body(): pl.pallas_call(place_results, out_shape=out_shape, in_specs=[anywhere] *...  1.98 us

profile of v4, /device:TPU:1, one launch (start us, length us, event | category | flops | bytes accessed | tf_op | source)
XLA Modules:
  0.0 92.2 jit_solution(13540529686068047677)
XLA Ops:
  0.6 89.6 %whole.1 = (bf16[256,2048]{1,0:T(8,128)(2,1)S(1)}, bf16[256,1024]{1,0:T(8,128)(2,1)S(1)}, bf16[256,1024]{1,0:T(8,128)(2,1)S(1)}, bf16[256,1024]{1,0:T(8,128)(2,1...) custom-call(bf16[256,2048]{1,0:T(8,128)(2,1)} %bitcast.14, ...), custom_call_target="tpu_custom_call" | custom-call | tf_op jit(solution)/shard_map/whole/pallas_call | solution.py:636
  90.2 2.0 %place.1 = (bf16[256,2048]{1,0:T(8,128)(2,1)}, bf16[256,1024]{1,0:T(8,128)(2,1)}, bf16[256,1024]{1,0:T(8,128)(2,1)}, bf16[256,1024]{1,0:T(8,128)(2,1)}, bf16[256...) custom-call(bf16[256,2048]{1,0:T(8,128)(2,1)S(1)} %get-tuple-element.24.refs_0_, ...), custom_call_target="tpu_custom_call" | custom-call | tf_op jit(solution)/shard_map/place/pallas_call | solution.py:648
